TPU v7x, 32 devices: a whole 2x2x4 slice. The times are simulated.
32 devices in a mesh: gx: 4 (over z), gy: 4 (over x, core), gz: 2 (over y).
Axes of the slice: x: 2, y: 2, z: 4, core: 2. Of those that a mesh axis runs over, the one named last changes fastest.
Arguments:
- composition: float32 [106, 8, 16, 256], P(None, 'gx', 'gy', 'gz'), may hold values from -6 to 6
- inv_temp: bfloat16 [8, 16, 256], P('gx', 'gy', 'gz'), may hold values from 0.3984375 to 1.59375
- diffusivity: float32 [106], replicated, may hold values from 0.01 to 0.1
- reactant_orders: bfloat16 [420, 106], replicated, may hold values from 0 to 0.019897461
- net_stoich: bfloat16 [106, 420], replicated, may hold values from -0.3125 to 0.3125
- log_rate: float32 [420], replicated, may hold values from -1 to 1
- activation: float32 [420], replicated, may hold values from 0.5 to 3
- hot_blocks: int32 [4, 4, 2, 8], P('gx', 'gy', 'gz'), may hold values from 0 to 7, as said below
- hot_counts: int32 [4, 4, 2], P('gx', 'gy', 'gz'), may hold values from 1 to 8, as said below
Outputs:
- composition_next: float32 [106, 8, 16, 256], P(None, 'gx', 'gy', 'gz')
Inputs may be any that keep to these rules, and one draw needn't show every extreme that they name: `hot_blocks`: each device's row holds 8 distinct block numbers of that device. `hot_counts`: some device has exactly 8 hot blocks.
All inputs are finite; a program needn't handle non-finite values.
Results may differ from a plain program's by a relative error of at most 0.0015.
Values may be sent and summed in bfloat16 or wider, within the bound.
A program may use at most 64 MiB of HBM per device.

v0:
```python
import jax
import jax.numpy as jnp
from jax import lax
from jax.sharding import PartitionSpec as P

SECTIONS = 4


rate_step = 0.5
blocks_group = 4


def extended(cells, sides, width):
    for axis, dim in sides:
        count = lax.axis_size(axis)
        head = lax.slice_in_dim(cells, 0, width, axis=dim)
        tail = lax.slice_in_dim(cells, cells.shape[dim] - width, cells.shape[dim], axis=dim)
        cells = jnp.concatenate(
            [
                lax.ppermute(tail, axis, [(i, (i + 1) % count) for i in range(count)]),
                cells,
                lax.ppermute(head, axis, [((i + 1) % count, i) for i in range(count)]),
            ],
            axis=dim,
        )
    return cells


def fourth_order(padded, axis_number, length):

    def window(offset):
        return lax.slice_in_dim(padded, offset, offset + length, axis=axis_number)

    return (16.0 * (window(1) + window(3)) - window(0) - window(4) - 30.0 * window(2)) / 12.0


def transport(field_in, diffusivity):
    field_shape = field_in.shape
    along_x = extended(field_in, (("gx", 1),), 2)
    along_y = extended(field_in, (("gy", 2),), 2)
    along_z = extended(field_in, (("gz", 3),), 2)
    laplace_sum = (
        fourth_order(along_x, 1, field_shape[1])
        + fourth_order(along_y, 2, field_shape[2])
        + fourth_order(along_z, 3, field_shape[3])
    )
    return field_in + diffusivity[:, None, None, None] * laplace_sum


def react_cells(columns, inverse, reactant_orders, net_stoich, log_rate, activation):
    initial = columns.astype(jnp.float32)
    current = initial
    operand = columns
    inverse_cells = inverse.astype(jnp.float32)
    for repeat in range(SECTIONS):
        logits = (
            jnp.dot(reactant_orders, operand, preferred_element_type=jnp.float32)
            + log_rate[:, None]
            - activation[:, None] * inverse_cells[None, :]
        )
        progress = jnp.exp(logits).astype(jnp.bfloat16)
        produced = jnp.dot(net_stoich, progress, preferred_element_type=jnp.float32)
        consumed = lax.dot_general(
            reactant_orders, progress, (((0,), (0,)), ((), ())), preferred_element_type=jnp.float32
        )
        current = current + rate_step * produced / (1.0 + rate_step * consumed)
        operand = current.astype(jnp.bfloat16)
    return (current - initial).astype(jnp.bfloat16)


def body(
    composition,
    inv_temp,
    diffusivity,
    reactant_orders,
    net_stoich,
    log_rate,
    activation,
    hot_blocks,
    hot_counts,
):
    species, cells_x, cells_y, cells_z = composition.shape
    blocks_total = cells_x * cells_y
    carried = transport(composition, diffusivity)
    hot_count = hot_blocks.shape[-1]
    listed = hot_blocks.reshape(hot_count)
    live_count = hot_counts.reshape(())
    is_valid = jnp.arange(hot_count, dtype=jnp.int32) < live_count
    flat_field = carried.reshape(species, blocks_total, cells_z)
    chosen = jnp.take(flat_field, listed, axis=1).astype(jnp.bfloat16)
    heat_rows = jnp.take(inv_temp.reshape(blocks_total, cells_z), listed, axis=0)
    heat_rows = jnp.where(is_valid[:, None], heat_rows, jnp.zeros_like(heat_rows))
    inverse_rows = heat_rows
    block_cells = chosen.shape[2]

    def advance(group_index, result):
        first_slot = group_index * blocks_group
        slot_piece = lax.dynamic_slice_in_dim(chosen, first_slot, blocks_group, 1)
        inverse = lax.dynamic_slice_in_dim(inverse_rows, first_slot, blocks_group, 0)
        increment = react_cells(
            slot_piece.reshape(species, blocks_group * block_cells),
            inverse.reshape(blocks_group * block_cells),
            reactant_orders,
            net_stoich,
            log_rate,
            activation,
        )
        return lax.dynamic_update_slice_in_dim(
            result, increment.reshape(species, blocks_group, block_cells), first_slot, 1
        )

    groups = (live_count + blocks_group - 1) // blocks_group
    result = lax.fori_loop(0, groups, advance, jnp.zeros_like(chosen))
    increments = jnp.where(is_valid[None, :, None], result.astype(jnp.float32), 0.0)
    flat_field = flat_field.at[:, listed, :].add(increments)
    return transport(flat_field.reshape(composition.shape), diffusivity)


def solution(mesh):
    in_specs = (
        P(None, "gx", "gy", "gz"),
        P("gx", "gy", "gz"),
        P(),
        P(),
        P(),
        P(),
        P(),
        P("gx", "gy", "gz", None),
        P("gx", "gy", "gz"),
    )
    out_specs = P(None, "gx", "gy", "gz")
    return jax.shard_map(body, mesh=mesh, in_specs=in_specs, out_specs=out_specs, check_vma=False)
```

profile of v0, /device:TPU:0, one launch (start us, length us, event | category | flops | bytes accessed | tf_op | source)
XLA Modules:
  0.0 71.9 jit_solution(10865775807422594499)
XLA Ops:
  0.0 3.0 %collective-permute-start = (f32[106,2,4,128]{3,2,1,0:T(4,128)}, f32[106,2,4,128]{3,2,1,0:T(4,128)S(1)}, u32[]{:S(2)}, u32[]{:S(2)}) collective-permute-start(f32[106,2,4,128]{3,2,1,0:T(4,128)} %param.11), channel_id=1, source_target_pairs={{0,8},{8,16},{16,24},{24,0},{1,9},{9,17},{17,25},{25,1},{2,10},{10... | collective-permute-start | bytes 1302536 | tf_op jit(solution)/shard_map/ppermute | solution.py:20
  3.0 2.1 %collective-permute-start.1 = (f32[106,2,4,128]{3,2,1,0:T(4,128)}, f32[106,2,4,128]{3,2,1,0:T(4,128)S(1)}, u32[]{:S(2)}, u32[]{:S(2)}) collective-permute-start(f32[106,2,4,128]{3,2,1,0:T(4,128)} %param.11), channel_id=1, source_target_pairs={{8,0},{16,8},{24,16},{0,24},{9,1},{17,9},{25,17},{1,25},{10,2},{18... | collective-permute-start | bytes 1302536 | tf_op jit(solution)/shard_map/ppermute | solution.py:22
  5.1 1.5 %fusion.78 = (f32[106,2,4,2]{3,2,1,0:T(4,128)S(1)}, f32[106,2,4,2]{3,2,1,0:T(4,128)S(1)}) fusion(f32[106,2,4,128]{3,2,1,0:T(4,128)} %param.11), kind=kLoop, calls=%fused_computation.137 | loop fusion | bytes 27136 | tf_op jit(solution)/shard_map/slice | solution.py:17
  6.6 1.7 %collective-permute-start.5 = (f32[106,2,4,2]{3,2,1,0:T(4,128)S(1)}, f32[106,2,4,2]{3,2,1,0:T(4,128)S(1)}, u32[]{:S(2)}, u32[]{:S(2)}) collective-permute-start(f32[106,2,4,2]{3,2,1,0:T(4,128)S(1)} %get-tuple-element.90), channel_id=1, source_target_pairs={{1,0},{0,1},{3,2},{2,3},{5,4},{4,5},{7,6},{6,7},{9,8},{8,9},{11,10... | collective-permute-start | bytes 20360 | tf_op jit(solution)/shard_map/ppermute | solution.py:22
  8.4 0.9 %fusion.77 = (f32[106,2,2,128]{3,2,1,0:T(2,128)}, f32[106,2,2,128]{3,2,1,0:T(2,128)}) fusion(f32[106,2,4,128]{3,2,1,0:T(4,128)S(1)} %copy-done.2), kind=kLoop, calls=%fused_computation.136 | loop fusion | bytes 868352 | tf_op jit(solution)/shard_map/slice | solution.py:17
  9.3 1.7 %collective-permute-start.3 = (f32[106,2,2,128]{3,2,1,0:T(2,128)}, f32[106,2,2,128]{3,2,1,0:T(2,128)}, u32[]{:S(2)}, u32[]{:S(2)}) collective-permute-start(f32[106,2,2,128]{3,2,1,0:T(2,128)} %get-tuple-element.88), channel_id=1, source_target_pairs={{2,0},{4,2},{6,4},{0,6},{3,1},{5,3},{7,5},{1,7},{10,8},{12,10},{14... | collective-permute-start | bytes 651272 | tf_op jit(solution)/shard_map/ppermute | solution.py:22
  11.7 0.6 gather_fusion.1
  12.4 0.6 copy-done.7
  13.1 5.1 %collective-permute-done.5 = f32[106,2,4,2]{3,2,1,0:T(4,128)S(1)} collective-permute-done((f32[106,2,4,2]{3,2,1,0:T(4,128)S(1)}, f32[106,2,4,2]{3,2,1,0:T(4,128)S(1)}, u32[]{:S(2)}, u32[]{:S(2)}) %collective-permute-start.5) | collective-permute-done | bytes 6816 | tf_op jit(solution)/shard_map/ppermute | solution.py:22
  18.1 1.5 %collective-permute-start.4 = (f32[106,2,4,2]{3,2,1,0:T(4,128)S(1)}, f32[106,2,4,2]{3,2,1,0:T(4,128)S(1)}, u32[]{:S(2)}, u32[]{:S(2)}) collective-permute-start(f32[106,2,4,2]{3,2,1,0:T(4,128)S(1)} %get-tuple-element.89), channel_id=1, source_target_pairs={{0,1},{1,0},{2,3},{3,2},{4,5},{5,4},{6,7},{7,6},{8,9},{9,8},{10,11... | collective-permute-start | bytes 20360 | tf_op jit(solution)/shard_map/ppermute | solution.py:20
  19.8 8.9 %collective-permute-done.4 = f32[106,2,4,2]{3,2,1,0:T(4,128)S(1)} collective-permute-done((f32[106,2,4,2]{3,2,1,0:T(4,128)S(1)}, f32[106,2,4,2]{3,2,1,0:T(4,128)S(1)}, u32[]{:S(2)}, u32[]{:S(2)}) %collective-permute-start.4) | collective-permute-done | bytes 6816 | tf_op jit(solution)/shard_map/ppermute | solution.py:20
  28.7 2.9 %multiply_add_fusion.1 = f32[106,2,4,128]{3,2,1,0:T(4,128)S(1)} fusion(f32[106,2,4,128]{3,2,1,0:T(4,128)S(1)} %copy-done.2, f32[106,2,4,130]{3,2,1,0:T(4,128)S(1)} %constant_dynamic-update-slice_fusion.1, f32[106,2,4,2]{3,2,1,0:T(4,128)S(1)} %collective-permute-done.4, f32[106,2,2,128]{3,2,1,0:T(2,128)} %collective-permute-done.3, ...), kind=kLoop, calls=%fused_computation.119 | loop fusion | flops 3039232 | bytes 3046440 | tf_op jit(solution)/shard_map/add | solution.py:47
  31.7 0.6 gather_fusion
  32.6 0.5 copy-done.5
  33.5 7.5 %while.10 = (s32[]{:T(128)}, bf16[106,8,128]{2,1,0:T(8,128)(2,1)S(1)}, s32[]{:T(128)}, bf16[106,8,128]{2,1,0:T(8,128)(2,1)S(1)}, bf16[420,106]{1,0:T(8,128)(2,1)...) while((s32[]{:T(128)}, ...), condition=%wide.region_1.2_spmd, body=%wide.region_0.1_spmd.sunk | while | flops 551968256 | bytes 11482881 | solution.py:113
  34.5 0.3 fusion.163
  38.3 0.3 fusion.163
  39.1 0.3 fusion.166
  41.2 1.2 %scatter_fusion = f32[106,8,128]{2,0,1:T(8,128)S(1)} fusion(f32[106,8,128]{2,0,1:T(8,128)S(1)} %bitcast.162, s32[8]{0:T(128)S(1)} %fusion.74, f32[8,106,128]{2,1,0:T(8,128)S(1)} %copy.12), kind=kCustom, calls=%fused_computation.2 | custom fusion | flops 108544 | bytes 1302560 | tf_op jit(solution)/shard_map/scatter-add | solution.py:115
  42.7 3.8 %collective-permute-start.7 = (f32[106,2,4,128]{3,2,1,0:T(4,128)S(1)}, f32[106,2,4,128]{3,2,1,0:T(4,128)S(1)}, u32[]{:S(2)}, u32[]{:S(2)}) collective-permute-start(f32[106,2,4,128]{3,2,1,0:T(4,128)S(1)} %get-tuple-element.82), channel_id=1, source_target_pairs={{8,0},{16,8},{24,16},{0,24},{9,1},{17,9},{25,17},{1,25},{10,2},{18... | collective-permute-start | bytes 1302536 | tf_op jit(solution)/shard_map/ppermute | solution.py:22
  46.8 1.7 %collective-permute-start.9 = (f32[106,2,2,128]{3,2,1,0:T(2,128)S(1)}, f32[106,2,2,128]{3,2,1,0:T(2,128)S(1)}, u32[]{:S(2)}, u32[]{:S(2)}) collective-permute-start(f32[106,2,2,128]{3,2,1,0:T(2,128)S(1)} %get-tuple-element.84), channel_id=1, source_target_pairs={{2,0},{4,2},{6,4},{0,6},{3,1},{5,3},{7,5},{1,7},{10,8},{12,10},{14... | collective-permute-start | bytes 651272 | tf_op jit(solution)/shard_map/ppermute | solution.py:22
  48.9 10.7 %collective-permute-done.11 = f32[106,2,4,2]{3,2,1,0:T(4,128)S(1)} collective-permute-done((f32[106,2,4,2]{3,2,1,0:T(4,128)S(1)}, f32[106,2,4,2]{3,2,1,0:T(4,128)S(1)}, u32[]{:S(2)}, u32[]{:S(2)}) %collective-permute-start.11) | collective-permute-done | bytes 6816 | tf_op jit(solution)/shard_map/ppermute | solution.py:22
  60.0 9.4 %collective-permute-done.10 = f32[106,2,4,2]{3,2,1,0:T(4,128)S(1)} collective-permute-done((f32[106,2,4,2]{3,2,1,0:T(4,128)S(1)}, f32[106,2,4,2]{3,2,1,0:T(4,128)S(1)}, u32[]{:S(2)}, u32[]{:S(2)}) %collective-permute-start.10) | collective-permute-done | bytes 6816 | tf_op jit(solution)/shard_map/ppermute | solution.py:20
  69.4 2.5 %multiply_add_fusion = f32[106,2,4,128]{3,2,1,0:T(4,128)} fusion(f32[106,2,4,128]{3,2,1,0:T(4,128)S(1)} %get-tuple-element.82, f32[106,2,4,130]{3,2,1,0:T(4,128)S(1)} %constant_dynamic-update-slice_fusion.3, f32[106,2,4,2]{3,2,1,0:T(4,128)S(1)} %collective-permute-done.10, f32[106,2,2,128]{3,2,1,0:T(2,128)S(1)} %collective-permute-done.9, ...), kind=kLoop, calls=%fused_computation.118 | loop fusion | flops 3039232 | bytes 3046440 | tf_op jit(solution)/shard_map/add | solution.py:47
  (77 shorter events, 8.7 us)
Async XLA Ops:
  0.0 11.7 %copy-start = (bf16[2,4,128]{2,1,0:T(4,128)(2,1)S(1)}, bf16[2,4,128]{2,1,0:T(4,128)(2,1)}, u32[]{:S(2)}) copy-start(bf16[2,4,128]{2,1,0:T(4,128)(2,1)} %param.12) | copy-start | bytes 6148
  0.0 8.4 %copy-start.2 = (f32[106,2,4,128]{3,2,1,0:T(4,128)S(1)}, f32[106,2,4,128]{3,2,1,0:T(4,128)}, u32[]{:S(2)}) copy-start(f32[106,2,4,128]{3,2,1,0:T(4,128)} %param.11) | copy-start | bytes 1302532
  0.0 28.7 %collective-permute-start = (f32[106,2,4,128]{3,2,1,0:T(4,128)}, f32[106,2,4,128]{3,2,1,0:T(4,128)S(1)}, u32[]{:S(2)}, u32[]{:S(2)}) collective-permute-start(f32[106,2,4,128]{3,2,1,0:T(4,128)} %param.11), channel_id=1, source_target_pairs={{0,8},{8,16},{16,24},{24,0},{1,9},{9,17},{17,25},{25,1},{2,10},{10... | collective-permute-start | bytes 1302536 | tf_op jit(solution)/shard_map/ppermute | solution.py:20
  3.0 25.7 %collective-permute-start.1 = (f32[106,2,4,128]{3,2,1,0:T(4,128)}, f32[106,2,4,128]{3,2,1,0:T(4,128)S(1)}, u32[]{:S(2)}, u32[]{:S(2)}) collective-permute-start(f32[106,2,4,128]{3,2,1,0:T(4,128)} %param.11), channel_id=1, source_target_pairs={{8,0},{16,8},{24,16},{0,24},{9,1},{17,9},{25,17},{1,25},{10,2},{18... | collective-permute-start | bytes 1302536 | tf_op jit(solution)/shard_map/ppermute | solution.py:22
  6.6 11.5 %collective-permute-start.5 = (f32[106,2,4,2]{3,2,1,0:T(4,128)S(1)}, f32[106,2,4,2]{3,2,1,0:T(4,128)S(1)}, u32[]{:S(2)}, u32[]{:S(2)}) collective-permute-start(f32[106,2,4,2]{3,2,1,0:T(4,128)S(1)} %get-tuple-element.90), channel_id=1, source_target_pairs={{1,0},{0,1},{3,2},{2,3},{5,4},{4,5},{7,6},{6,7},{9,8},{8,9},{11,10... | collective-permute-start | bytes 20360 | tf_op jit(solution)/shard_map/ppermute | solution.py:22
  9.3 19.4 %collective-permute-start.2 = (f32[106,2,2,128]{3,2,1,0:T(2,128)}, f32[106,2,2,128]{3,2,1,0:T(2,128)}, u32[]{:S(2)}, u32[]{:S(2)}) collective-permute-start(f32[106,2,2,128]{3,2,1,0:T(2,128)} %get-tuple-element.87), channel_id=1, source_target_pairs={{0,2},{2,4},{4,6},{6,0},{1,3},{3,5},{5,7},{7,1},{8,10},{10,12},{12... | collective-permute-start | bytes 651272 | tf_op jit(solution)/shard_map/ppermute | solution.py:20
  9.3 2.4 %copy-start.3 = (s32[1,1,1,8]{3,2,1,0:T(1,128)S(1)}, s32[1,1,1,8]{3,2,1,0:T(1,128)}, u32[]{:S(2)}) copy-start(s32[1,1,1,8]{3,2,1,0:T(1,128)} %param.18) | copy-start | bytes 100
  9.3 19.4 %collective-permute-start.3 = (f32[106,2,2,128]{3,2,1,0:T(2,128)}, f32[106,2,2,128]{3,2,1,0:T(2,128)}, u32[]{:S(2)}, u32[]{:S(2)}) collective-permute-start(f32[106,2,2,128]{3,2,1,0:T(2,128)} %get-tuple-element.88), channel_id=1, source_target_pairs={{2,0},{4,2},{6,4},{0,6},{3,1},{5,3},{7,5},{1,7},{10,8},{12,10},{14... | collective-permute-start | bytes 651272 | tf_op jit(solution)/shard_map/ppermute | solution.py:22
  12.3 0.7 copy-start.7
  18.1 10.5 %collective-permute-start.4 = (f32[106,2,4,2]{3,2,1,0:T(4,128)S(1)}, f32[106,2,4,2]{3,2,1,0:T(4,128)S(1)}, u32[]{:S(2)}, u32[]{:S(2)}) collective-permute-start(f32[106,2,4,2]{3,2,1,0:T(4,128)S(1)} %get-tuple-element.89), channel_id=1, source_target_pairs={{0,1},{1,0},{2,3},{3,2},{4,5},{5,4},{6,7},{7,6},{8,9},{9,8},{10,11... | collective-permute-start | bytes 20360 | tf_op jit(solution)/shard_map/ppermute | solution.py:20
  32.5 0.7 copy-start.5
  32.5 0.7 copy-start.6
  32.5 0.9 %copy-start.1 = (bf16[420,106]{1,0:T(8,128)(2,1)S(1)}, bf16[420,106]{1,0:T(8,128)(2,1)}, u32[]{:S(2)}) copy-start(bf16[420,106]{1,0:T(8,128)(2,1)} %param.14) | copy-start | bytes 267124
  32.6 0.9 %copy-start.4 = (bf16[106,420]{0,1:T(8,128)(2,1)S(1)}, bf16[106,420]{0,1:T(8,128)(2,1)}, u32[]{:S(2)}) copy-start(bf16[106,420]{0,1:T(8,128)(2,1)} %param.15) | copy-start | bytes 267124
  42.7 26.7 %collective-permute-start.6 = (f32[106,2,4,128]{3,2,1,0:T(4,128)S(1)}, f32[106,2,4,128]{3,2,1,0:T(4,128)S(1)}, u32[]{:S(2)}, u32[]{:S(2)}) collective-permute-start(f32[106,2,4,128]{3,2,1,0:T(4,128)S(1)} %get-tuple-element.82), channel_id=1, source_target_pairs={{0,8},{8,16},{16,24},{24,0},{1,9},{9,17},{17,25},{25,1},{2,10},{10... | collective-permute-start | bytes 1302536 | tf_op jit(solution)/shard_map/ppermute | solution.py:20
  42.7 26.7 %collective-permute-start.7 = (f32[106,2,4,128]{3,2,1,0:T(4,128)S(1)}, f32[106,2,4,128]{3,2,1,0:T(4,128)S(1)}, u32[]{:S(2)}, u32[]{:S(2)}) collective-permute-start(f32[106,2,4,128]{3,2,1,0:T(4,128)S(1)} %get-tuple-element.82), channel_id=1, source_target_pairs={{8,0},{16,8},{24,16},{0,24},{9,1},{17,9},{25,17},{1,25},{10,2},{18... | collective-permute-start | bytes 1302536 | tf_op jit(solution)/shard_map/ppermute | solution.py:22
  46.7 22.7 %collective-permute-start.8 = (f32[106,2,2,128]{3,2,1,0:T(2,128)S(1)}, f32[106,2,2,128]{3,2,1,0:T(2,128)S(1)}, u32[]{:S(2)}, u32[]{:S(2)}) collective-permute-start(f32[106,2,2,128]{3,2,1,0:T(2,128)S(1)} %get-tuple-element.83), channel_id=1, source_target_pairs={{0,2},{2,4},{4,6},{6,0},{1,3},{3,5},{5,7},{7,1},{8,10},{10,12},{12... | collective-permute-start | bytes 651272 | tf_op jit(solution)/shard_map/ppermute | solution.py:20
  46.8 22.6 %collective-permute-start.9 = (f32[106,2,2,128]{3,2,1,0:T(2,128)S(1)}, f32[106,2,2,128]{3,2,1,0:T(2,128)S(1)}, u32[]{:S(2)}, u32[]{:S(2)}) collective-permute-start(f32[106,2,2,128]{3,2,1,0:T(2,128)S(1)} %get-tuple-element.84), channel_id=1, source_target_pairs={{2,0},{4,2},{6,4},{0,6},{3,1},{5,3},{7,5},{1,7},{10,8},{12,10},{14... | collective-permute-start | bytes 651272 | tf_op jit(solution)/shard_map/ppermute | solution.py:22
  48.8 10.8 %collective-permute-start.11 = (f32[106,2,4,2]{3,2,1,0:T(4,128)S(1)}, f32[106,2,4,2]{3,2,1,0:T(4,128)S(1)}, u32[]{:S(2)}, u32[]{:S(2)}) collective-permute-start(f32[106,2,4,2]{3,2,1,0:T(4,128)S(1)} %get-tuple-element.86), channel_id=1, source_target_pairs={{1,0},{0,1},{3,2},{2,3},{5,4},{4,5},{7,6},{6,7},{9,8},{8,9},{11,10... | collective-permute-start | bytes 20360 | tf_op jit(solution)/shard_map/ppermute | solution.py:22
  59.6 9.8 %collective-permute-start.10 = (f32[106,2,4,2]{3,2,1,0:T(4,128)S(1)}, f32[106,2,4,2]{3,2,1,0:T(4,128)S(1)}, u32[]{:S(2)}, u32[]{:S(2)}) collective-permute-start(f32[106,2,4,2]{3,2,1,0:T(4,128)S(1)} %get-tuple-element.85), channel_id=1, source_target_pairs={{0,1},{1,0},{2,3},{3,2},{4,5},{5,4},{6,7},{7,6},{8,9},{9,8},{10,11... | collective-permute-start | bytes 20360 | tf_op jit(solution)/shard_map/ppermute | solution.py:20
where the time goes:
time: 72.4 us; the launch traced here: 71.9 us
  waiting for transfers between devices  34.1 us (47%)
  starting transfers between devices  16.1 us (22%)
  other arithmetic  6.99 us (10%)
  local copies, waits for them, and re-layouts  6.77 us (9%)
  matrix products  6.73 us (9%)
  between operations  0.91 us (1%)
    ppermute x6, waiting for transfers between devices, extended(): lax.ppermute(tail, axis, [(i, (i + 1) % count) for i in range(count)])  18.3 us
    ppermute x6, waiting for transfers between devices, extended(): lax.ppermute(head, axis, [((i + 1) % count, i) for i in range(count)])  15.8 us
    ppermute x6, starting transfers between devices, extended(): lax.ppermute(head, axis, [((i + 1) % count, i) for i in range(count)])  11.2 us
    add x2, other arithmetic, transport(): return field_in + diffusivity[:, None, None, None] * laplace_sum  5.45 us
    ppermute x6, starting transfers between devices, extended(): lax.ppermute(tail, axis, [(i, (i + 1) % count) for i in range(count)])  4.95 us
    slice x4, local copies, waits for them, and re-layouts, extended(): lax.slice_in_dim(cells, cells.shape[dim] - width, cells.shape[dim], axis=...  2.87 us
    dot_general x8, matrix products, react_cells(): jnp.dot(reactant_orders, operand, preferred_element_type=jnp.float32)  2.45 us
    dot_general x8, matrix products, react_cells(): produced = jnp.dot(net_stoich, progress, preferred_element_type=jnp.float32)  2.17 us
  transfers between devices with their start and end apart: 12, of which 4 were waited for; matrix products, arithmetic and copies ran while one was open for 5% of the time, Pallas kernels for 0%

commit v1 on v0

v1 whole, which is shorter than its diff:
```python
import functools

import jax
import jax.numpy as jnp
from jax import lax
from jax.experimental import pallas as pl
from jax.experimental.pallas import tpu as pltpu
from jax.sharding import PartitionSpec as P

SECTIONS = 4
MESH = pl.DeviceIdType.MESH
F32, BF16 = jnp.float32, jnp.bfloat16
GROUP = 1


def up(value, step):
    return (value + step - 1) // step * step


def kernel(
    cells_x, cells_y, species, reactions,
    comp_ref, inv_ref, diff_ref, orders_ref, net_ref, rate_ref, act_ref, blocks_ref, counts_ref,
    out_ref,
    field, send, edges_out, from_low_x, from_high_x, from_low_y, from_high_y, edges_low, edges_high,
    orders_pad, orders_t, logit_w, gain_w,
    sems_x, sems_y, sems_z,
):
    size_x, size_y, size_z = (lax.axis_size(a) for a in ("gx", "gy", "gz"))
    rows = field.shape[3]
    lanes = field.shape[4]
    blocks = cells_x * cells_y

    def beside(axis, size, step):
        return {axis: lax.rem(lax.axis_index(axis) + (step + size), size)}

    low_x, high_x = beside("gx", size_x, -1), beside("gx", size_x, 1)
    low_y, high_y = beside("gy", size_y, -1), beside("gy", size_y, 1)
    low_z, high_z = beside("gz", size_z, -1), beside("gz", size_z, 1)
    others = [low_x, high_x, low_y, high_y, high_z] + ([low_z] if size_z > 2 else [])

    barrier = pltpu.get_barrier_semaphore()
    for other in others:
        pl.semaphore_signal(barrier, inc=1, device_id=other, device_id_type=MESH)

    lane = lax.broadcasted_iota(jnp.int32, (rows, lanes), 1)
    edge = (lane < 2) | (lane >= lanes - 2)
    place = lane % 4

    def number(x, y):
        return x * cells_y + y

    def copy(src, dst, sems, index, target):
        return pltpu.make_async_remote_copy(
            src_ref=src, dst_ref=dst, send_sem=sems.at[0, index], recv_sem=sems.at[1, index],
            device_id=target, device_id_type=MESH,
        )

    def x_copies(stage, y):
        base = (stage * cells_y + y) * 2
        return [
            copy(send.at[stage, y, pl.ds(cells_x - 2, 2)], from_low_x.at[stage, y], sems_x, base, high_x),
            copy(send.at[stage, y, pl.ds(0, 2)], from_high_x.at[stage, y], sems_x, base + 1, low_x),
        ]

    def y_copies(stage):
        made = {}
        for k in range(2):
            base = (stage * 2 + k) * 2
            made.setdefault(cells_y - 2 + k, []).append(
                copy(send.at[stage, cells_y - 2 + k], from_low_y.at[stage, k], sems_y, base, high_y)
            )
            made.setdefault(k, []).append(
                copy(send.at[stage, k], from_high_y.at[stage, k], sems_y, base + 1, low_y)
            )
        return made

    def y_low(stage, k):
        return copy(send.at[stage, cells_y - 2 + k], from_low_y.at[stage, k], sems_y, (stage * 2 + k) * 2, high_y)

    def y_high(stage, k):
        return copy(send.at[stage, k], from_high_y.at[stage, k], sems_y, (stage * 2 + k) * 2 + 1, low_y)

    def z_copies(stage):
        made = [copy(edges_out.at[stage], edges_low.at[stage], sems_z, stage * 2, high_z)]
        if size_z > 2:
            made.append(copy(edges_out.at[stage], edges_high.at[stage], sems_z, stage * 2 + 1, low_z))
        return made

    def pack(value, index):
        return pltpu.roll(value, (4 * index + 2) % lanes, 1)

    def edge_terms(stage, own):
        low = edges_low[stage].astype(F32)
        got = low if size_z == 2 else jnp.where(place >= 2, edges_high[stage].astype(F32), low)
        d = got - own
        far = jnp.where(place < 2, pltpu.roll(d, lanes - 2, 1), pltpu.roll(d, 2, 1))
        near = jnp.where(place == 1, pltpu.roll(d, lanes - 1, 1), pltpu.roll(d, 1, 1))
        return jnp.where((place == 1) | (place == 2), 16.0 * near, 0.0) - far

    def at_x(stage, x, y):
        if x < 0:
            return from_low_x[stage, y, 2 + x].astype(F32)
        if x >= cells_x:
            return from_high_x[stage, y, x - cells_x].astype(F32)
        return field[stage, y, x]

    def at_y(stage, x, y):
        if y < 0:
            return from_low_y[stage, 2 + y, x].astype(F32)
        if y >= cells_y:
            return from_high_y[stage, y - cells_y, x].astype(F32)
        return field[stage, y, x]

    def diffuse(stage, x, y, scale, terms):
        v = field[stage, y, x]
        near = (
            at_x(stage, x - 1, y) + at_x(stage, x + 1, y) + at_y(stage, x, y - 1) + at_y(stage, x, y + 1)
            + pltpu.roll(v, 1, 1) + pltpu.roll(v, lanes - 1, 1)
        )
        far = (
            at_x(stage, x - 2, y) + at_x(stage, x + 2, y) + at_y(stage, x, y - 2) + at_y(stage, x, y + 2)
            + pltpu.roll(v, 2, 1) + pltpu.roll(v, lanes - 2, 1)
        )
        index = number(x, y)
        fix = jnp.where(edge, pltpu.roll(terms, (2 * lanes - 4 * index - 2) % lanes, 1), 0.0)
        return v + scale * (16.0 * near - far - 90.0 * v + fix)

    packed = jnp.zeros((rows, lanes), F32)
    for y in range(cells_y):
        for x in range(cells_x):
            field[0, y, x, pl.ds(species // 8 * 8, rows - species // 8 * 8), :] = jnp.zeros(
                (rows - species // 8 * 8, lanes), F32
            )
            field[0, y, x, pl.ds(0, species), :] = comp_ref[pl.ds(number(x, y), species, stride=blocks), :]
            v = field[0, y, x]
            send[0, y, x] = v.astype(BF16)
            packed = jnp.where(lane // 4 == number(x, y), pack(v, number(x, y)), packed)
    edges_out[0] = packed.astype(BF16)

    pl.semaphore_wait(barrier, len(others))
    waits_send = []

    def start(copies):
        for c in copies:
            c.start()
            waits_send.append(c)

    first_x = [x_copies(0, y) for y in range(cells_y)]
    first_y = y_copies(0)
    first_z = z_copies(0)
    start(first_z)
    for y in range(cells_y):
        start(first_x[y])
        start(first_y.get(y, []))

    wide = orders_t.shape[1]
    orders_pad[...] = jnp.zeros_like(orders_pad)
    orders_pad[pl.ds(0, reactions), pl.ds(0, species)] = orders_ref[...].astype(F32)
    transposed = orders_pad[...].T
    used = logit_w.shape[0]
    gain_w[...] = jnp.zeros_like(gain_w)
    gain_w[pl.ds(0, species), pl.ds(0, reactions)] = (0.5 * net_ref[...].astype(F32)).astype(BF16)
    gain_w[pl.ds(rows, rows), :] = (0.5 * transposed[:rows, :used]).astype(BF16)
    orders_t[...] = transposed
    for k, (ref, sign) in enumerate(((rate_ref, 1.0), (act_ref, -1.0))):
        value = sign * ref[...]
        upper = value.astype(BF16).astype(F32)
        orders_t[pl.ds(species + 2 * k, 1), pl.ds(0, reactions)] = upper
        orders_t[pl.ds(species + 2 * k + 1, 1), pl.ds(0, reactions)] = value - upper
    logit_w[...] = orders_t[...].T[:used, :rows].astype(BF16)
    number_row = diff_ref[...] * (1.0 / 12.0)
    orders_pad[pl.ds(0, lanes), :] = jnp.zeros((lanes, orders_pad.shape[1]), F32)
    orders_pad[pl.ds(0, lanes), pl.ds(0, species)] = jnp.broadcast_to(number_row, (lanes, species))
    scale = orders_pad[pl.ds(0, lanes), :].T[:rows, :]

    inverse = inv_ref[...].astype(F32)
    count = counts_ref[0]
    hot = []
    for index in range(blocks):
        found = jnp.int32(0)
        for k in range(blocks_ref.shape[0]):
            found = found + jnp.where((blocks_ref[k] == index) & (count > k), 1, 0)
        hot.append(found)
    tile = species // 8 * 8
    row = lax.broadcasted_iota(jnp.int32, (rows - tile, lanes), 0) + tile

    def react(columns):
        begin = jnp.concatenate(columns, axis=1)
        operand = begin.astype(BF16)
        begin = operand.astype(F32)
        current = begin
        for _ in range(SECTIONS):
            logits = jnp.dot(logit_w[...], operand, preferred_element_type=F32)
            progress = jnp.exp(logits).astype(BF16)
            both = jnp.dot(gain_w[...], progress, preferred_element_type=F32)
            current = current + both[:rows] / (1.0 + both[rows:])
            operand = current.astype(BF16)
        return (current - begin).astype(BF16).astype(F32)

    for c in first_z:
        c.wait_recv()
    terms = edge_terms(0, packed)
    packed = jnp.zeros((rows, lanes), F32)
    second_x = [x_copies(1, y) for y in range(cells_y)]
    second_y = y_copies(1)
    second_z = z_copies(1)
    done_low, done_high = set(), set()

    def wait_y(stage, copies, y, done):
        for k in range(2):
            for low in (True, False):
                need = y - 2 <= k - 2 if low else y + 2 >= cells_y + k
                if need and (low, k) not in done:
                    done.add((low, k))
                    (y_low if low else y_high)(stage, k).wait_recv()

    for first in range(0, cells_y, GROUP):
        columns, carried, places = [], [], []
        for y in range(first, min(first + GROUP, cells_y)):
            for c in first_x[y]:
                c.wait_recv()
            wait_y(0, first_y, y, done_low)
            for x in range(cells_x):
                v = diffuse(0, x, y, scale, terms)
                heat = jnp.broadcast_to(inverse[x, y : y + 1, :], (rows - tile, lanes))
                last = jnp.where(row < species, v[tile:], 0.0)
                last = jnp.where((row >= species) & (row < species + 2), 1.0, last)
                last = jnp.where((row >= species + 2) & (row < species + 4), heat, last)
                columns.append(jnp.concatenate([v[:tile], last], axis=0))
                carried.append(v)
                places.append((x, y))
        increment = react(columns)
        for k, (x, y) in enumerate(places):
            index = number(x, y)
            is_hot = jnp.broadcast_to(hot[index], (rows, lanes)) > 0
            v = carried[k] + jnp.where(is_hot, increment[:, k * lanes : (k + 1) * lanes], 0.0)
            field[1, y, x] = v
            send[1, y, x] = v.astype(BF16)
            packed = jnp.where(lane // 4 == index, pack(v, index), packed)
        for y in range(first, min(first + GROUP, cells_y)):
            start(second_x[y])
            start(second_y.get(y, []))
    edges_out[1] = packed.astype(BF16)
    start(second_z)

    for c in second_z:
        c.wait_recv()
    terms = edge_terms(1, packed)
    for y in range(cells_y):
        for c in second_x[y]:
            c.wait_recv()
        wait_y(1, second_y, y, done_high)
        for x in range(cells_x):
            v = diffuse(1, x, y, scale, terms)
            out_ref[pl.ds(number(x, y), species, stride=blocks), :] = v[:species]
    for c in waits_send:
        c.wait_send()


def body(
    composition, inv_temp, diffusivity, reactant_orders, net_stoich, log_rate, activation, hot_blocks, hot_counts
):
    species, cells_x, cells_y, lanes = composition.shape
    reactions = reactant_orders.shape[0]
    blocks = cells_x * cells_y
    rows = up(species + 4, 16)
    used = up(reactions, 16)
    tall, broad = up(reactions, 128), up(rows, 128)
    vmem, smem = pl.BlockSpec(memory_space=pltpu.VMEM), pl.BlockSpec(memory_space=pltpu.SMEM)
    out = pl.pallas_call(
        functools.partial(kernel, cells_x, cells_y, species, reactions),
        out_shape=jax.ShapeDtypeStruct((species * blocks, lanes), F32),
        in_specs=[vmem] * 7 + [smem] * 2,
        out_specs=vmem,
        scratch_shapes=[
            pltpu.VMEM((2, cells_y, cells_x, rows, lanes), F32),
            pltpu.VMEM((2, cells_y, cells_x, rows, lanes), BF16),
            pltpu.VMEM((2, rows, lanes), BF16),
            pltpu.VMEM((2, cells_y, 2, rows, lanes), BF16),
            pltpu.VMEM((2, cells_y, 2, rows, lanes), BF16),
            pltpu.VMEM((2, 2, cells_x, rows, lanes), BF16),
            pltpu.VMEM((2, 2, cells_x, rows, lanes), BF16),
            pltpu.VMEM((2, rows, lanes), BF16),
            pltpu.VMEM((2, rows, lanes), BF16),
            pltpu.VMEM((tall, broad), F32),
            pltpu.VMEM((broad, tall), F32),
            pltpu.VMEM((used, rows), BF16),
            pltpu.VMEM((2 * rows, used), BF16),
            pltpu.SemaphoreType.DMA((2, 4 * cells_y)),
            pltpu.SemaphoreType.DMA((2, 8)),
            pltpu.SemaphoreType.DMA((2, 4)),
        ],
        compiler_params=pltpu.CompilerParams(
            collective_id=0, has_side_effects=True, vmem_limit_bytes=32 * 2**20
        ),
        cost_estimate=pl.CostEstimate(
            flops=2 * SECTIONS * 3 * reactions * species * blocks * lanes,
            bytes_accessed=8 * species * blocks * lanes,
            transcendentals=SECTIONS * reactions * blocks * lanes,
        ),
    )(
        composition.reshape(species * blocks, lanes),
        inv_temp,
        diffusivity.reshape(1, species),
        reactant_orders,
        net_stoich,
        log_rate.reshape(1, reactions),
        activation.reshape(1, reactions),
        hot_blocks.reshape(-1),
        hot_counts.reshape(1),
    )
    return out.reshape(composition.shape)


def solution(mesh):
    in_specs = (
        P(None, "gx", "gy", "gz"),
        P("gx", "gy", "gz"),
        P(), P(), P(), P(), P(),
        P("gx", "gy", "gz", None),
        P("gx", "gy", "gz"),
    )
    return jax.shard_map(
        body, mesh=mesh, in_specs=in_specs, out_specs=P(None, "gx", "gy", "gz"), check_vma=False
    )
```

time: 72.4 us -> 31.7 us (0.44)
  waiting for transfers between devices: 34.1 us -> 0 us
  Pallas kernels: 0 us -> 27.8 us
  starting transfers between devices: 16.1 us -> 0 us
  other arithmetic: 6.99 us -> 0 us
  matrix products: 6.73 us -> 0 us
  local copies, waits for them, and re-layouts: 6.77 us -> 2.9 us
    ppermute x12 -> x0, waiting for transfers between devices: 34.1 us -> none  [the longest x6 18.3 us: extended(): lax.ppermute(tail, axis, [(i, (i + 1) % count) for i in range(count)])]
    pallas_call x0 -> x1, Pallas kernels: none -> 27.8 us  [body(): pl.pallas_call(functools.partial(kernel, cells_x, cells_y, species, react...]
    ppermute x12 -> x0, starting transfers between devices: 16.1 us -> none  [the longest x6 11.2 us: extended(): lax.ppermute(head, axis, [((i + 1) % count, i) for i in range(count)])]
    dot_general x24 -> x0, matrix products: 6.73 us -> none  [the longest x8 2.45 us: react_cells(): jnp.dot(reactant_orders, operand, preferred_element_type=jnp.float32)]
    add x2 -> x0, other arithmetic: 5.45 us -> none  [transport(): return field_in + diffusivity[:, None, None, None] * laplace_sum]
    slice x4 -> x0, local copies, waits for them, and re-layouts: 2.87 us -> none  [extended(): lax.slice_in_dim(cells, cells.shape[dim] - width, cells.shape[dim], axis=...]
    scatter-add x1 -> x0, other arithmetic: 1.22 us -> none  [body(): flat_field = flat_field.at[:, listed, :].add(increments)]
    gather x2 -> x0, local copies, waits for them, and re-layouts: 1.15 us -> none  [the longest x1 0.59 us: body(): chosen = jnp.take(flat_field, listed, axis=1).astype(jnp.bfloat16)]
  transfers between devices with their start and end apart: 12 -> 0, of which waited for: 4 -> 0; matrix products, arithmetic and copies ran while one was open for 5% -> 0% of each run, Pallas kernels for 0% -> 0%
where the time goes in v1:
time: 31.7 us; the launch traced here: 31.5 us
  Pallas kernels  27.8 us (88%)
  local copies, waits for them, and re-layouts  2.9 us (9%)
  between operations  0.76 us (2%)
    pallas_call x1, Pallas kernels, body(): pl.pallas_call(functools.partial(kernel, cells_x, cells_y, species, react...  27.8 us
    unnamed x16, local copies, waits for them, and re-layouts  2.9 us

profile of v1, /device:TPU:0, one launch (start us, length us, event | category | flops | bytes accessed | tf_op | source)
XLA Modules:
  0.0 31.5 jit_solution(13595423480786361542)
XLA Ops:
  0.7 0.0 copy-start.1
  0.7 0.0 copy-start.2
  0.7 0.0 copy-start.3
  0.7 0.0 copy-start.4
  0.7 0.0 copy-start.5
  0.7 0.0 copy-start.6
  0.7 1.1 %copy.10.net_ref = bf16[106,420]{1,0:T(8,128)(2,1)S(1)} copy(bf16[106,420]{0,1:T(8,128)(2,1)} %param.13) | data formatting | bytes 178080 | tf_op args[4]
  1.8 0.0 copy-done.1
  1.8 0.0 copy-done.2
  1.8 0.0 copy-done.3
  1.9 0.0 copy-done.4
  1.9 0.0 copy-done.5
  1.9 0.0 copy-done.6
  1.9 0.0 copy-start
  1.9 1.0 %copy-done = f32[106,2,4,128]{3,2,1,0:T(4,128)S(1)} copy-done((f32[106,2,4,128]{3,2,1,0:T(4,128)S(1)}, f32[106,2,4,128]{3,2,1,0:T(4,128)}, u32[]{:S(2)}) %copy-start) | copy-done | bytes 434200
  2.9 27.8 %shard_map.91 = f32[848,128]{1,0:T(8,128)S(1)} custom-call(f32[848,128]{1,0:T(8,128)S(1)} %bitcast.9, bf16[2,4,128]{2,1,0:T(4,128)(2,1)S(1)} %copy-done.2, f32[1,106]{1,0:T(1,128)S(1)} %bitcast.12, bf16[420,106]{1,0:T(8,128)(2,1)S(1)} %copy-done.1, bf16[106,420]{1,0:T(8,128)(2,1)S(1)} %copy.10.net_ref, f32[1,420]{1,0:T(1,128)S(1)} %bitcast.10, ...), custom_call_target="tpu_custom_call" | custom-call | flops 1094123520 | bytes 868352 | tf_op jit(solution)/shard_map/pallas_call | solution.py:270
  30.8 0.8 %copy.13 = f32[106,2,4,128]{3,2,1,0:T(4,128)} copy(f32[106,2,4,128]{3,2,1,0:T(4,128)S(1)} %bitcast.8) | data formatting | bytes 868352
Async XLA Ops:
  0.7 1.2 %copy-start.1 = (bf16[420,106]{1,0:T(8,128)(2,1)S(1)}, bf16[420,106]{1,0:T(8,128)(2,1)}, u32[]{:S(2)}) copy-start(bf16[420,106]{1,0:T(8,128)(2,1)} %orders_ref.1) | copy-start | bytes 267124
  0.7 1.2 %copy-start.2 = (bf16[2,4,128]{2,1,0:T(4,128)(2,1)S(1)}, bf16[2,4,128]{2,1,0:T(4,128)(2,1)}, u32[]{:S(2)}) copy-start(bf16[2,4,128]{2,1,0:T(4,128)(2,1)} %inv_ref.1) | copy-start | bytes 6148
  0.7 1.2 %copy-start.3 = (f32[420]{0:T(512)S(1)}, f32[420]{0:T(512)}, u32[]{:S(2)}) copy-start(f32[420]{0:T(512)} %param.14) | copy-start | bytes 5044
  0.7 1.2 %copy-start.4 = (f32[420]{0:T(512)S(1)}, f32[420]{0:T(512)}, u32[]{:S(2)}) copy-start(f32[420]{0:T(512)} %param.15) | copy-start | bytes 5044
  0.7 1.2 %copy-start.5 = (f32[106]{0:T(128)S(1)}, f32[106]{0:T(128)}, u32[]{:S(2)}) copy-start(f32[106]{0:T(128)} %param.11) | copy-start | bytes 1276
  0.7 1.2 %copy-start.6 = (s32[1,1,1,8]{3,2,1,0:T(1,128)S(1)}, s32[1,1,1,8]{3,2,1,0:T(1,128)}, u32[]{:S(2)}) copy-start(s32[1,1,1,8]{3,2,1,0:T(1,128)} %param.16) | copy-start | bytes 100
  1.9 1.0 %copy-start = (f32[106,2,4,128]{3,2,1,0:T(4,128)S(1)}, f32[106,2,4,128]{3,2,1,0:T(4,128)}, u32[]{:S(2)}) copy-start(f32[106,2,4,128]{3,2,1,0:T(4,128)} %param.9) | copy-start | bytes 1302532

commit v2 on v1

--- a/solution.py
+++ b/solution.py
@@ -19,11 +19,12 @@
 
 def kernel(
     cells_x, cells_y, species, reactions,
-    comp_ref, inv_ref, diff_ref, orders_ref, net_ref, rate_ref, act_ref, blocks_ref, counts_ref,
+    comp_hbm, inv_hbm, diff_hbm, orders_hbm, net_hbm, rate_hbm, act_hbm, blocks_hbm, counts_hbm,
     out_ref,
     field, send, edges_out, from_low_x, from_high_x, from_low_y, from_high_y, edges_low, edges_high,
     orders_pad, orders_t, logit_w, gain_w,
-    sems_x, sems_y, sems_z,
+    comp, inv_ref, diff_ref, orders_ref, net_ref, rate_ref, act_ref, blocks_ref, counts_ref,
+    sems_x, sems_y, sems_z, sems_in,
 ):
     size_x, size_y, size_z = (lax.axis_size(a) for a in ("gx", "gy", "gz"))
     rows = field.shape[3]
@@ -41,6 +42,15 @@
     barrier = pltpu.get_barrier_semaphore()
     for other in others:
         pl.semaphore_signal(barrier, inc=1, device_id=other, device_id_type=MESH)
+    loads = [
+        pltpu.make_async_copy(src, dst, sems_in.at[k])
+        for k, (src, dst) in enumerate((
+            (comp_hbm, comp), (orders_hbm, orders_ref), (net_hbm, net_ref), (inv_hbm, inv_ref), (diff_hbm, diff_ref),
+            (rate_hbm, rate_ref), (act_hbm, act_ref), (blocks_hbm, blocks_ref), (counts_hbm, counts_ref),
+        ))
+    ]
+    for load in loads:
+        load.start()
 
     lane = lax.broadcasted_iota(jnp.int32, (rows, lanes), 1)
     edge = (lane < 2) | (lane >= lanes - 2)
@@ -125,19 +135,6 @@
         fix = jnp.where(edge, pltpu.roll(terms, (2 * lanes - 4 * index - 2) % lanes, 1), 0.0)
         return v + scale * (16.0 * near - far - 90.0 * v + fix)
 
-    packed = jnp.zeros((rows, lanes), F32)
-    for y in range(cells_y):
-        for x in range(cells_x):
-            field[0, y, x, pl.ds(species // 8 * 8, rows - species // 8 * 8), :] = jnp.zeros(
-                (rows - species // 8 * 8, lanes), F32
-            )
-            field[0, y, x, pl.ds(0, species), :] = comp_ref[pl.ds(number(x, y), species, stride=blocks), :]
-            v = field[0, y, x]
-            send[0, y, x] = v.astype(BF16)
-            packed = jnp.where(lane // 4 == number(x, y), pack(v, number(x, y)), packed)
-    edges_out[0] = packed.astype(BF16)
-
-    pl.semaphore_wait(barrier, len(others))
     waits_send = []
 
     def start(copies):
@@ -148,20 +145,34 @@
     first_x = [x_copies(0, y) for y in range(cells_y)]
     first_y = y_copies(0)
     first_z = z_copies(0)
-    start(first_z)
+    loads[0].wait()
+    packed = jnp.zeros((rows, lanes), F32)
+    tile = species // 8 * 8
     for y in range(cells_y):
+        for x in range(cells_x):
+            field[0, y, x, pl.ds(tile, rows - tile), :] = jnp.zeros((rows - tile, lanes), F32)
+            field[0, y, x, pl.ds(0, species), :] = comp[pl.ds(number(x, y), species, stride=blocks), :]
+            send[0, y, x] = field[0, y, x].astype(BF16)
+        if y == 0:
+            pl.semaphore_wait(barrier, len(others))
         start(first_x[y])
         start(first_y.get(y, []))
-
-    wide = orders_t.shape[1]
+    for y in range(cells_y):
+        for x in range(cells_x):
+            packed = jnp.where(lane // 4 == number(x, y), pack(field[0, y, x], number(x, y)), packed)
+    edges_out[0] = packed.astype(BF16)
+    start(first_z)
+    for load in loads[1:]:
+        load.wait()
+
     orders_pad[...] = jnp.zeros_like(orders_pad)
     orders_pad[pl.ds(0, reactions), pl.ds(0, species)] = orders_ref[...].astype(F32)
+    used = logit_w.shape[0]
     transposed = orders_pad[...].T
-    used = logit_w.shape[0]
-    gain_w[...] = jnp.zeros_like(gain_w)
-    gain_w[pl.ds(0, species), pl.ds(0, reactions)] = (0.5 * net_ref[...].astype(F32)).astype(BF16)
     gain_w[pl.ds(rows, rows), :] = (0.5 * transposed[:rows, :used]).astype(BF16)
     orders_t[...] = transposed
+    orders_pad[pl.ds(0, reactions), pl.ds(0, species)] = net_ref[...].astype(F32)
+    gain_w[pl.ds(0, rows), :] = (0.5 * orders_pad[...].T[:rows, :used]).astype(BF16)
     for k, (ref, sign) in enumerate(((rate_ref, 1.0), (act_ref, -1.0))):
         value = sign * ref[...]
         upper = value.astype(BF16).astype(F32)
@@ -174,14 +185,11 @@
     scale = orders_pad[pl.ds(0, lanes), :].T[:rows, :]
 
     inverse = inv_ref[...].astype(F32)
-    count = counts_ref[0]
-    hot = []
-    for index in range(blocks):
-        found = jnp.int32(0)
-        for k in range(blocks_ref.shape[0]):
-            found = found + jnp.where((blocks_ref[k] == index) & (count > k), 1, 0)
-        hot.append(found)
-    tile = species // 8 * 8
+    listed = blocks_ref[...]
+    valid = lax.broadcasted_iota(jnp.int32, listed.shape, 1) < counts_ref[0]
+    hot = [
+        jnp.sum(jnp.where(valid & (listed == index), 1.0, 0.0), axis=1, keepdims=True) for index in range(blocks)
+    ]
     row = lax.broadcasted_iota(jnp.int32, (rows - tile, lanes), 0) + tile
 
     def react(columns):
@@ -232,7 +240,7 @@
         increment = react(columns)
         for k, (x, y) in enumerate(places):
             index = number(x, y)
-            is_hot = jnp.broadcast_to(hot[index], (rows, lanes)) > 0
+            is_hot = jnp.broadcast_to(hot[index], (rows, lanes)) > 0.5
             v = carried[k] + jnp.where(is_hot, increment[:, k * lanes : (k + 1) * lanes], 0.0)
             field[1, y, x] = v
             send[1, y, x] = v.astype(BF16)
@@ -266,12 +274,11 @@
     rows = up(species + 4, 16)
     used = up(reactions, 16)
     tall, broad = up(reactions, 128), up(rows, 128)
-    vmem, smem = pl.BlockSpec(memory_space=pltpu.VMEM), pl.BlockSpec(memory_space=pltpu.SMEM)
     out = pl.pallas_call(
         functools.partial(kernel, cells_x, cells_y, species, reactions),
         out_shape=jax.ShapeDtypeStruct((species * blocks, lanes), F32),
-        in_specs=[vmem] * 7 + [smem] * 2,
-        out_specs=vmem,
+        in_specs=[pl.BlockSpec(memory_space=pltpu.HBM)] * 9,
+        out_specs=pl.BlockSpec(memory_space=pltpu.VMEM),
         scratch_shapes=[
             pltpu.VMEM((2, cells_y, cells_x, rows, lanes), F32),
             pltpu.VMEM((2, cells_y, cells_x, rows, lanes), BF16),
@@ -286,12 +293,22 @@
             pltpu.VMEM((broad, tall), F32),
             pltpu.VMEM((used, rows), BF16),
             pltpu.VMEM((2 * rows, used), BF16),
+            pltpu.VMEM((species * blocks, lanes), F32),
+            pltpu.VMEM(inv_temp.shape, BF16),
+            pltpu.VMEM((1, species), F32),
+            pltpu.VMEM((reactions, species), BF16),
+            pltpu.VMEM((reactions, species), BF16),
+            pltpu.VMEM((1, reactions), F32),
+            pltpu.VMEM((1, reactions), F32),
+            pltpu.VMEM((1, hot_blocks.shape[-1]), jnp.int32),
+            pltpu.VMEM((1, 1, 1), jnp.int32),
             pltpu.SemaphoreType.DMA((2, 4 * cells_y)),
             pltpu.SemaphoreType.DMA((2, 8)),
             pltpu.SemaphoreType.DMA((2, 4)),
+            pltpu.SemaphoreType.DMA((9,)),
         ],
         compiler_params=pltpu.CompilerParams(
-            collective_id=0, has_side_effects=True, vmem_limit_bytes=32 * 2**20
+            collective_id=0, has_side_effects=True, vmem_limit_bytes=60 * 2**20
         ),
         cost_estimate=pl.CostEstimate(
             flops=2 * SECTIONS * 3 * reactions * species * blocks * lanes,
@@ -303,11 +320,11 @@
         inv_temp,
         diffusivity.reshape(1, species),
         reactant_orders,
-        net_stoich,
+        net_stoich.T,
         log_rate.reshape(1, reactions),
         activation.reshape(1, reactions),
-        hot_blocks.reshape(-1),
-        hot_counts.reshape(1),
+        hot_blocks.reshape(1, -1),
+        hot_counts,
     )
     return out.reshape(composition.shape)
 

time: 31.7 us -> 30.8 us (0.972)
  local copies, waits for them, and re-layouts: 2.9 us -> 1.8 us
  Pallas kernels: 27.8 us -> 28.2 us
    unnamed x16 -> x1, local copies, waits for them, and re-layouts: 2.9 us -> 1.8 us
    pallas_call x1, Pallas kernels: 27.8 us -> 28.2 us  [body(): pl.pallas_call(functools.partial(kernel, cells_x, cells_y, species, react...]
where the time goes in v2:
time: 30.8 us; the launch traced here: 30.6 us
  Pallas kernels  28.2 us (92%)
  local copies, waits for them, and re-layouts  1.8 us (6%)
  between operations  0.66 us (2%)
    pallas_call x1, Pallas kernels, body(): pl.pallas_call(functools.partial(kernel, cells_x, cells_y, species, react...  28.2 us
    unnamed x1, local copies, waits for them, and re-layouts  1.8 us

profile of v2, /device:TPU:0, one launch (start us, length us, event | category | flops | bytes accessed | tf_op | source)
XLA Modules:
  0.0 30.6 jit_solution(17804229566990371803)
XLA Ops:
  0.7 28.2 %shard_map.91 = f32[848,128]{1,0:T(8,128)} custom-call(f32[848,128]{1,0:T(8,128)} %bitcast.8, bf16[2,4,128]{2,1,0:T(4,128)(2,1)} %inv_hbm.1, f32[1,106]{1,0:T(1,128)} %bitcast.12, bf16[420,106]{1,0:T(8,128)(2,1)} %orders_hbm.1, bf16[420,106]{1,0:T(8,128)(2,1)} %bitcast.9, f32[1,420]{1,0:T(1,128)} %bitcast.10, f32[1,420]{1,0:T(1,128)} %bitcast.11, ...), custom_call_target="tpu_custom_call" | custom-call | flops 1094123520 | bytes 868352 | tf_op jit(solution)/shard_map/pallas_call | solution.py:277
  28.8 1.8 %copy.12 = f32[106,2,4,128]{3,2,1,0:T(4,128)} copy(f32[106,2,4,128]{3,2,1,0:T(4,128)} %bitcast.7) | data formatting | bytes 868352
